TPU v7x, 32 devices: a whole 2x2x4 slice. The times are simulated.
32 devices in a mesh: groups: 2 (over y), space: 4 (over x, core), contour: 4 (over z).
Axes of the slice: x: 2, y: 2, z: 4, core: 2. Of those that a mesh axis runs over, the one named last changes fastest.
Arguments:
- body_force: float32 [6, 16, 1024], P('groups', 'space'), parts along dimension 0, may hold values from -6 to 6
- ice_thickness: float32 [2048], P('groups'), parts along dimension 0, may hold values from 0.5 to 4
- ice_mask: int32 [2048], P('groups'), parts along dimension 0, may hold values 0 or 1
- layer_ids: int32 [16, 1024], P('space'), may hold values from 0 to 3
- shear_modulus: float32 [4], replicated, may hold values from 0.5 to 4
- relax_rate: float32 [4], replicated, may hold values from 0.2 to 5
- node_ids: int32 [12], P('contour'), may hold values from 0 to 11, each once
- time_ids: int32 [24], P('groups'), parts along dimension 0, may hold values from 0 to 63
Outputs:
- laplace_field: float32 [24, 6, 16, 1024], P(('groups', 'contour'), None, 'space'), parts along dimension 0
- surface_motion: float32 [24, 3, 1024], P('groups', None, ('space', 'contour')), parts along dimension 0
There are 2 independent parts, one for each index of `groups`. A program takes and returns all parts, laid end to end along the dimension named above; an argument that names none is the same for every part. Nothing has to cross between parts.
Inputs may be any that keep to these rules, and one draw needn't show every extreme that they name: `node_ids`: every contour node appears in exactly one slot.
All inputs are finite; a program needn't handle non-finite values.
Results may differ from a plain program's by a relative error of at most 0.00007.
Values sent between devices are 32-bit elements; how exact they have to be, the bound alone decides.
A program may use at most 64 MiB of HBM per device.

v0:
```python
import math

import jax
import jax.numpy as jnp
from jax import lax
from jax.sharding import PartitionSpec as P

HX = 128
T_STEPS = 64
COARSE_SWEEPS = 8


OMEGA = 0.7
KAPPA = 1.0


def extended(x, sides, width):
    for axis, dim in sides:
        count, length = (lax.axis_size(axis), x.shape[dim])
        up = [(i, (i + 1) % count) for i in range(count - 1)]
        down = [(j, i) for i, j in up]
        last = lax.slice_in_dim(x, length - width, length, axis=dim)
        first = lax.slice_in_dim(x, 0, width, axis=dim)
        before = lax.ppermute(last, axis, up)
        after = lax.ppermute(first, axis, down)
        x = jnp.concatenate([before, x, after], axis=dim)
    return x


def contour_nodes(node_ids, node_count):
    angles = -math.pi + (node_ids.astype(jnp.float32) + 0.5) * (2.0 * math.pi / node_count)
    contour_scale = 0.5 * node_count
    sine_theta = jnp.sin(angles)
    cotangent = jnp.cos(angles) / sine_theta
    pole_real = contour_scale * (0.5017 * angles * cotangent - 0.4622)
    pole_imag = contour_scale * 0.2645 * angles
    slope_real = contour_scale * 0.5017 * (cotangent - angles / (sine_theta * sine_theta))
    weight_real = contour_scale * 0.2645 / node_count + 0.0 * angles
    weight_imag = -slope_real / node_count
    return (pole_real, pole_imag, weight_real, weight_imag)


def layer_tables(pole_real, pole_imag, shear_modulus, relax_rate):
    pole_r = pole_real[:, None]
    pole_i = pole_imag[:, None]
    shifted_real = pole_r + relax_rate[None, :]
    denominator = shifted_real * shifted_real + pole_i * pole_i
    ratio_real = (pole_r * shifted_real + pole_i * pole_i) / denominator
    ratio_imag = (pole_i * shifted_real - pole_r * pole_i) / denominator
    shear_real = shear_modulus[None, :] * ratio_real
    shear_imag = shear_modulus[None, :] * ratio_imag
    shear_size = shear_modulus[None, :] * jnp.sqrt(
        (pole_r * pole_r + pole_i * pole_i) / denominator
    )
    return (shear_real, shear_imag, shear_size)


def per_cell(tables, layer_ids):
    summed = jnp.zeros((tables.shape[0], 1) + layer_ids.shape, tables.dtype)
    for layer_index in range(tables.shape[1]):
        chosen = layer_ids == layer_index
        summed = summed + jnp.where(
            chosen[None, None], tables[:, layer_index, None, None, None], 0.0
        )
    return summed


def horizontal(values, row_width):
    last_size = values.shape[-1]
    column = jnp.arange(last_size) % row_width
    zero_column = jnp.zeros_like(values[..., :1])
    zero_rows = jnp.zeros_like(values[..., :row_width])
    from_left = jnp.where(
        column > 0, jnp.concatenate([zero_column, values[..., :-1]], axis=-1), 0.0
    )
    from_right = jnp.where(
        column < row_width - 1, jnp.concatenate([values[..., 1:], zero_column], axis=-1), 0.0
    )
    from_front = jnp.concatenate([zero_rows, values[..., :-row_width]], axis=-1)
    from_back = jnp.concatenate([values[..., row_width:], zero_rows], axis=-1)
    return from_left + from_right + from_front + from_back


def zero_pad(values):
    zero_layer = jnp.zeros_like(values[..., :1, :])
    return jnp.concatenate([zero_layer, values, zero_layer], axis=-2)


def operate(padded, shear_real, shear_imag, spacing_factor, row_width):
    center = padded[..., 1:-1, :]
    laplace_term = (
        6.0 * center - padded[..., :-2, :] - padded[..., 2:, :] - horizontal(center, row_width)
    ) * spacing_factor
    lap_real = laplace_term[..., :3, :, :]
    lap_imag = laplace_term[..., 3:, :, :]
    out_real = shear_real * lap_real - shear_imag * lap_imag + KAPPA * center[..., :3, :, :]
    out_imag = shear_real * lap_imag + shear_imag * lap_real + KAPPA * center[..., 3:, :, :]
    return jnp.concatenate([out_real, out_imag], axis=-3)


def complex_scale(gain_real, gain_imag, values):
    val_real = values[..., :3, :, :]
    val_imag = values[..., 3:, :, :]
    return jnp.concatenate(
        [gain_real * val_real - gain_imag * val_imag, gain_real * val_imag + gain_imag * val_real],
        axis=-3,
    )


def gains(shear_real, shear_imag, shear_size, stencil_factor):
    diagonal_real = stencil_factor * shear_real + KAPPA
    diagonal_imag = stencil_factor * shear_imag
    bound_value = stencil_factor * shear_size + KAPPA
    inverse = OMEGA / (bound_value * bound_value)
    return (diagonal_real * inverse, -diagonal_imag * inverse)


def restrict(values, row_width):
    column_pairs = values[..., 0::2] + values[..., 1::2]
    half_width = row_width // 2
    shaped = column_pairs.reshape(
        column_pairs.shape[:-1] + (column_pairs.shape[-1] // row_width, row_width)
    )
    row_pairs = shaped[..., :half_width] + shaped[..., half_width:]
    flat_cells = row_pairs.reshape(row_pairs.shape[:-2] + (-1,))
    depth_pairs = flat_cells.reshape(
        flat_cells.shape[:-2] + (flat_cells.shape[-2] // 2, 2, flat_cells.shape[-1])
    )
    return (depth_pairs[..., 0, :] + depth_pairs[..., 1, :]) * 0.125


def prolong(values, row_width):
    wide_copy = jnp.repeat(values, 2, axis=-1)
    shaped = wide_copy.reshape(wide_copy.shape[:-1] + (wide_copy.shape[-1] // row_width, row_width))
    tall_copy = jnp.concatenate([shaped, shaped], axis=-1)
    flat_cells = tall_copy.reshape(tall_copy.shape[:-2] + (-1,))
    return jnp.repeat(flat_cells, 2, axis=-2)


def per_device(
    body_force, ice_thickness, ice_mask, layer_ids, shear_modulus, relax_rate, node_ids, time_ids
):
    node_count = node_ids.shape[0] * lax.axis_size("contour")
    pole_real, pole_imag, weight_real, weight_imag = contour_nodes(node_ids, node_count)
    tables = layer_tables(pole_real, pole_imag, shear_modulus, relax_rate)
    is_top = lax.axis_index("space") == 0
    ice_load = -ice_thickness * ice_mask.astype(jnp.float32)
    pole_square = pole_real * pole_real + pole_imag * pole_imag
    inverse_real = (pole_real / pole_square)[:, None, None, None]
    inverse_imag = (-pole_imag / pole_square)[:, None, None, None]
    shear_real = per_cell(tables[0], layer_ids)
    shear_imag = per_cell(tables[1], layer_ids)
    shear_size = per_cell(tables[2], layer_ids)
    forcing_base = body_force.at[0, 0, :].add(jnp.where(is_top, ice_load, 0.0))
    forcing = jnp.concatenate(
        [forcing_base[None] * inverse_real, forcing_base[None] * inverse_imag], axis=1
    )
    gain_real, gain_imag = gains(shear_real, shear_imag, shear_size, 6.0)

    def residual(field):
        padded = extended(field, (("space", 2),), 1)
        return forcing - operate(padded, shear_real, shear_imag, 1.0, HX)

    field = complex_scale(gain_real, gain_imag, forcing)
    field = field + complex_scale(gain_real, gain_imag, residual(field))
    fine_residual = residual(field)
    coarse_rhs = restrict(fine_residual, HX)
    coarse_real = restrict(shear_real, HX)
    coarse_imag = restrict(shear_imag, HX)
    coarse_size = restrict(shear_size, HX)
    half_width = HX // 2
    coarse_depth = coarse_rhs.shape[2]
    stacked = jnp.concatenate([coarse_real, coarse_imag, coarse_size], axis=1)
    whole_residual, whole_moduli = (
        lax.all_gather(coarse_rhs, "space", axis=2, tiled=True),
        lax.all_gather(stacked, "space", axis=2, tiled=True),
    )
    whole_real = whole_moduli[:, 0:1]
    whole_imag = whole_moduli[:, 1:2]
    whole_size = whole_moduli[:, 2:3]
    coarse_gr, coarse_gi = gains(whole_real, whole_imag, whole_size, 1.5)
    correction = complex_scale(coarse_gr, coarse_gi, whole_residual)
    for counter in range(COARSE_SWEEPS - 1):
        correction = correction + complex_scale(
            coarse_gr,
            coarse_gi,
            whole_residual
            - operate(zero_pad(correction), whole_real, whole_imag, 0.25, half_width),
        )
    leftover = whole_residual - operate(
        zero_pad(correction), whole_real, whole_imag, 0.25, half_width
    )
    correction = correction + jnp.mean(leftover, axis=2, keepdims=True) / KAPPA
    correction = lax.dynamic_slice_in_dim(
        correction, lax.axis_index("space") * coarse_depth, coarse_depth, axis=2
    )
    field = field + prolong(correction, HX)
    for counter in range(2):
        field = field + complex_scale(gain_real, gain_imag, residual(field))
    time_values = (time_ids.astype(jnp.float32) + 1.0) * (2.0 / T_STEPS)
    growth = jnp.exp(time_values[:, None] * pole_real[None, :])
    phase_angle = time_values[:, None] * pole_imag[None, :]
    factor_real = growth * (
        weight_real[None, :] * jnp.cos(phase_angle) - weight_imag[None, :] * jnp.sin(phase_angle)
    )
    factor_imag = growth * (
        weight_real[None, :] * jnp.sin(phase_angle) + weight_imag[None, :] * jnp.cos(phase_angle)
    )
    top_layer = field[:, :, 0, :]
    surface_term = jnp.einsum(
        "jk,kcs->jcs", factor_real, top_layer[:, :3], precision=lax.Precision.HIGHEST
    ) - jnp.einsum("jk,kcs->jcs", factor_imag, top_layer[:, 3:], precision=lax.Precision.HIGHEST)
    surface_term = jnp.where(is_top, surface_term, 0.0)
    surface_motion = lax.psum_scatter(
        surface_term, ("space", "contour"), scatter_dimension=2, tiled=True
    )
    return (field, surface_motion)


def solution(mesh):
    in_specs = (
        P("groups", "space", None),
        P("groups"),
        P("groups"),
        P("space", None),
        P(),
        P(),
        P("contour"),
        P("groups"),
    )
    out_specs = (
        P(("groups", "contour"), None, "space", None),
        P("groups", None, ("space", "contour")),
    )
    return jax.shard_map(
        per_device, mesh=mesh, in_specs=in_specs, out_specs=out_specs, check_vma=False
    )
```

profile of v0, /device:TPU:0, one launch (start us, length us, event | category | flops | bytes accessed | tf_op | source)
XLA Modules:
  0.0 152.7 jit_solution(12984507983256757717)
XLA Ops:
  7.2 0.8 copy.79
  8.0 0.7 negate_multiply_fusion.2
  8.7 0.7 fusion.112
  9.4 0.7 fusion.108
  10.1 0.8 fusion.90
  10.8 0.7 broadcast_compare_fusion.3
  11.6 0.7 multiply_select_fusion
  12.4 0.2 select_add_fusion.1
  13.0 2.4 %collective-permute-start = (f32[3,6,1,1024]{3,0,1,2:T(4,128)S(1)}, f32[3,6,1,1024]{3,0,1,2:T(4,128)S(1)}, u32[]{:S(2)}, u32[]{:S(2)}) collective-permute-start(f32[3,6,1,1024]{3,0,1,2:T(4,128)S(1)} %get-tuple-element.63), channel_id=1, source_target_pairs={{0,4},{4,8},{8,12},{1,5},{5,9},{9,13},{2,6},{6,10},{10,14},{3,7},{... | collective-permute-start | bytes 221192 | tf_op jit(solution)/shard_map/ppermute | solution.py:24
  15.3 1.3 collective-permute-start.1
  16.6 0.3 fusion.1
  17.2 0.9 slice.635
  18.1 0.9 slice.636
  19.0 0.9 slice.641
  19.9 0.9 slice.642
  20.8 0.9 slice.647
  21.7 0.9 slice.648
  23.4 8.2 %all_gather.6 = f32[3,3,8,256]{3,1,2,0:T(4,128)S(1)} all-gather(f32[3,3,2,256]{3,1,2,0:T(4,128)S(1)} %pad_maximum_fusion.14), channel_id=1, replica_groups=mesh['groups'=2,'space'=4,'contour'=4] {'space'}, dimensions={2}, use_global_device_ids=true | all-gather | bytes 92160 | tf_op jit(solution)/shard_map/all_gather | solution.py:176
  31.8 0.4 fusion.13
  32.9 0.3 fusion.119
  33.2 2.3 %collective-permute-start.2 = (f32[3,6,1,1024]{3,0,1,2:T(4,128)S(1)}, f32[3,6,1,1024]{3,0,1,2:T(4,128)S(1)}, u32[]{:S(2)}, u32[]{:S(2)}) collective-permute-start(f32[3,6,1,1024]{3,0,1,2:T(4,128)S(1)} %get-tuple-element.57), channel_id=1, source_target_pairs={{0,4},{4,8},{8,12},{1,5},{5,9},{9,13},{2,6},{6,10},{10,14},{3,7},{... | collective-permute-start | bytes 221192 | tf_op jit(solution)/shard_map/ppermute | solution.py:24
  35.5 1.5 collective-permute-start.3
  37.1 2.8 %collective-permute-done.3 = f32[3,6,1,1024]{3,0,1,2:T(4,128)S(1)} collective-permute-done((f32[3,6,1,1024]{3,0,1,2:T(4,128)S(1)}, f32[3,6,1,1024]{3,0,1,2:T(4,128)S(1)}, u32[]{:S(2)}, u32[]{:S(2)}) %collective-permute-start.3) | collective-permute-done | bytes 73760 | tf_op jit(solution)/shard_map/ppermute | solution.py:25
  39.9 0.5 fusion.10
  40.7 5.3 %slice.667 = f32[3,6,4,512]{3,0,1,2:T(4,128)S(1)} slice(f32[3,6,4,1024]{3,0,1,2:T(4,128)S(1)} %maximum_subtract_fusion.1), slice={[0:3:1], [0:6:1], [0:4:1], [0:1024:2]} | slice | bytes 294912 | tf_op jit(solution)/shard_map/slice | solution.py:119
  46.0 5.3 %slice.668 = f32[3,6,4,512]{3,0,1,2:T(4,128)S(1)} slice(f32[3,6,4,1024]{3,0,1,2:T(4,128)S(1)} %maximum_subtract_fusion.1), slice={[0:3:1], [0:6:1], [0:4:1], [1:1024:2]} | slice | bytes 294912 | tf_op jit(solution)/shard_map/slice | solution.py:119
  51.9 7.4 %all-gather = f32[3,6,8,1,256]{4,3,2,1,0:T(1,128)S(1)} all-gather(f32[3,6,2,1,256]{4,3,2,1,0:T(1,128)S(1)} %fusion.59), channel_id=2, replica_groups=mesh['groups'=2,'space'=4,'contour'=4] {'space'}, dimensions={2}, use_global_device_ids=true | all-gather | bytes 184320 | tf_op jit(solution)/shard_map/all_gather | solution.py:175
  63.3 0.3 copy.32
  63.6 0.5 broadcast_in_dim.385
  64.2 0.5 copy.33
  65.1 0.3 fusion.116
  65.4 2.1 %collective-permute-start.4 = (f32[3,6,1,1024]{3,0,1,2:T(4,128)S(1)}, f32[3,6,1,1024]{3,0,1,2:T(4,128)S(1)}, u32[]{:S(2)}, u32[]{:S(2)}) collective-permute-start(f32[3,6,1,1024]{3,0,1,2:T(4,128)S(1)} %get-tuple-element.51), channel_id=1, source_target_pairs={{0,4},{4,8},{8,12},{1,5},{5,9},{9,13},{2,6},{6,10},{10,14},{3,7},{... | collective-permute-start | bytes 221192 | tf_op jit(solution)/shard_map/ppermute | solution.py:24
  67.5 1.3 collective-permute-start.5
  68.9 2.5 %collective-permute-done.5 = f32[3,6,1,1024]{3,0,1,2:T(4,128)S(1)} collective-permute-done((f32[3,6,1,1024]{3,0,1,2:T(4,128)S(1)}, f32[3,6,1,1024]{3,0,1,2:T(4,128)S(1)}, u32[]{:S(2)}, u32[]{:S(2)}) %collective-permute-start.5) | collective-permute-done | bytes 73760 | tf_op jit(solution)/shard_map/ppermute | solution.py:25
  71.4 0.4 fusion.7
  72.4 0.3 fusion.113
  72.8 5.1 %collective-permute-start.6 = (f32[3,6,1,1024]{3,0,1,2:T(4,128)S(1)}, f32[3,6,1,1024]{3,0,1,2:T(4,128)S(1)}, u32[]{:S(2)}, u32[]{:S(2)}) collective-permute-start(f32[3,6,1,1024]{3,0,1,2:T(4,128)S(1)} %get-tuple-element.45), channel_id=1, source_target_pairs={{0,4},{4,8},{8,12},{1,5},{5,9},{9,13},{2,6},{6,10},{10,14},{3,7},{... | collective-permute-start | bytes 221192 | tf_op jit(solution)/shard_map/ppermute | solution.py:24
  77.9 1.5 collective-permute-start.7
  79.6 1.6 %collective-permute-done.7 = f32[3,6,1,1024]{3,0,1,2:T(4,128)S(1)} collective-permute-done((f32[3,6,1,1024]{3,0,1,2:T(4,128)S(1)}, f32[3,6,1,1024]{3,0,1,2:T(4,128)S(1)}, u32[]{:S(2)}, u32[]{:S(2)}) %collective-permute-start.7) | collective-permute-done | bytes 73760 | tf_op jit(solution)/shard_map/ppermute | solution.py:25
  81.1 0.4 fusion.4
  82.2 0.5 fusion.57
  82.7 0.5 fusion
  83.2 0.9 copy.39
  84.1 1.5 reshape.329
  85.7 0.9 copy.36
  86.6 57.7 %reduce-scatter.4.cloned.1.call-done = f32[64,36]{1,0:T(8,128)} async-done(((f32[1024,36]{1,0:T(8,128)}), f32[64,36]{1,0:T(8,128)}) %reduce-scatter.4.cloned.1.call-update) | async-done | bytes 9232
  144.3 0.9 reshape.330
  145.2 0.7 copy.37
  (133 shorter events, 8.5 us)
Async XLA Ops:
  7.2 137.1 %reduce-scatter.4.cloned.1.call-start = ((), (), s32[]{:S(2)}) async-start(), calls=%async_computation.1 | async-start | bytes 557056
  12.9 18.8 %copy-start = (s32[12]{0:T(128)S(1)}, s32[12]{0:T(128)}, u32[]{:S(2)}) copy-start(s32[12]{0:T(128)} %param.17) | copy-start | bytes 148
  13.0 18.8 %collective-permute-start = (f32[3,6,1,1024]{3,0,1,2:T(4,128)S(1)}, f32[3,6,1,1024]{3,0,1,2:T(4,128)S(1)}, u32[]{:S(2)}, u32[]{:S(2)}) collective-permute-start(f32[3,6,1,1024]{3,0,1,2:T(4,128)S(1)} %get-tuple-element.63), channel_id=1, source_target_pairs={{0,4},{4,8},{8,12},{1,5},{5,9},{9,13},{2,6},{6,10},{10,14},{3,7},{... | collective-permute-start | bytes 221192 | tf_op jit(solution)/shard_map/ppermute | solution.py:24
  15.3 16.5 %collective-permute-start.1 = (f32[3,6,1,1024]{3,0,1,2:T(4,128)S(1)}, f32[3,6,1,1024]{3,0,1,2:T(4,128)S(1)}, u32[]{:S(2)}, u32[]{:S(2)}) collective-permute-start(f32[3,6,1,1024]{3,0,1,2:T(4,128)S(1)} %get-tuple-element.64), channel_id=1, source_target_pairs={{4,0},{8,4},{12,8},{5,1},{9,5},{13,9},{6,2},{10,6},{14,10},{7,3},{... | collective-permute-start | bytes 221192 | tf_op jit(solution)/shard_map/ppermute | solution.py:25
  33.2 3.8 %collective-permute-start.2 = (f32[3,6,1,1024]{3,0,1,2:T(4,128)S(1)}, f32[3,6,1,1024]{3,0,1,2:T(4,128)S(1)}, u32[]{:S(2)}, u32[]{:S(2)}) collective-permute-start(f32[3,6,1,1024]{3,0,1,2:T(4,128)S(1)} %get-tuple-element.57), channel_id=1, source_target_pairs={{0,4},{4,8},{8,12},{1,5},{5,9},{9,13},{2,6},{6,10},{10,14},{3,7},{... | collective-permute-start | bytes 221192 | tf_op jit(solution)/shard_map/ppermute | solution.py:24
  35.5 4.4 %collective-permute-start.3 = (f32[3,6,1,1024]{3,0,1,2:T(4,128)S(1)}, f32[3,6,1,1024]{3,0,1,2:T(4,128)S(1)}, u32[]{:S(2)}, u32[]{:S(2)}) collective-permute-start(f32[3,6,1,1024]{3,0,1,2:T(4,128)S(1)} %get-tuple-element.58), channel_id=1, source_target_pairs={{4,0},{8,4},{12,8},{5,1},{9,5},{13,9},{6,2},{10,6},{14,10},{7,3},{... | collective-permute-start | bytes 221192 | tf_op jit(solution)/shard_map/ppermute | solution.py:25
  65.4 3.5 %collective-permute-start.4 = (f32[3,6,1,1024]{3,0,1,2:T(4,128)S(1)}, f32[3,6,1,1024]{3,0,1,2:T(4,128)S(1)}, u32[]{:S(2)}, u32[]{:S(2)}) collective-permute-start(f32[3,6,1,1024]{3,0,1,2:T(4,128)S(1)} %get-tuple-element.51), channel_id=1, source_target_pairs={{0,4},{4,8},{8,12},{1,5},{5,9},{9,13},{2,6},{6,10},{10,14},{3,7},{... | collective-permute-start | bytes 221192 | tf_op jit(solution)/shard_map/ppermute | solution.py:24
  67.5 3.9 %collective-permute-start.5 = (f32[3,6,1,1024]{3,0,1,2:T(4,128)S(1)}, f32[3,6,1,1024]{3,0,1,2:T(4,128)S(1)}, u32[]{:S(2)}, u32[]{:S(2)}) collective-permute-start(f32[3,6,1,1024]{3,0,1,2:T(4,128)S(1)} %get-tuple-element.52), channel_id=1, source_target_pairs={{4,0},{8,4},{12,8},{5,1},{9,5},{13,9},{6,2},{10,6},{14,10},{7,3},{... | collective-permute-start | bytes 221192 | tf_op jit(solution)/shard_map/ppermute | solution.py:25
  72.8 6.8 %collective-permute-start.6 = (f32[3,6,1,1024]{3,0,1,2:T(4,128)S(1)}, f32[3,6,1,1024]{3,0,1,2:T(4,128)S(1)}, u32[]{:S(2)}, u32[]{:S(2)}) collective-permute-start(f32[3,6,1,1024]{3,0,1,2:T(4,128)S(1)} %get-tuple-element.45), channel_id=1, source_target_pairs={{0,4},{4,8},{8,12},{1,5},{5,9},{9,13},{2,6},{6,10},{10,14},{3,7},{... | collective-permute-start | bytes 221192 | tf_op jit(solution)/shard_map/ppermute | solution.py:24
  77.9 3.2 %collective-permute-start.7 = (f32[3,6,1,1024]{3,0,1,2:T(4,128)S(1)}, f32[3,6,1,1024]{3,0,1,2:T(4,128)S(1)}, u32[]{:S(2)}, u32[]{:S(2)}) collective-permute-start(f32[3,6,1,1024]{3,0,1,2:T(4,128)S(1)} %get-tuple-element.46), channel_id=1, source_target_pairs={{4,0},{8,4},{12,8},{5,1},{9,5},{13,9},{6,2},{10,6},{14,10},{7,3},{... | collective-permute-start | bytes 221192 | tf_op jit(solution)/shard_map/ppermute | solution.py:25
Sparse Core Ops, SparseCore 0:
  85.8 58.4 reduce-scatter.3
where the time goes:
time: 153 us
  waiting for transfers between devices  64.7 us (42%)
  local copies, waits for them, and re-layouts  26.7 us (17%)
  starting transfers between devices  17.4 us (11%)
  blocking collectives  15.6 us (10%)
  between operations  15.1 us (10%)
  other arithmetic  12.1 us (8%)
    unnamed x2, waiting for transfers between devices  57.8 us
    slice x8, local copies, waits for them, and re-layouts, restrict(): column_pairs = values[..., 0::2] + values[..., 1::2]  16 us
    ppermute x4, starting transfers between devices, extended(): before = lax.ppermute(last, axis, up)  11.8 us
    all_gather x1, blocking collectives, per_device(): lax.all_gather(stacked, 'space', axis=2, tiled=True)  8.21 us
    all_gather x1, blocking collectives, per_device(): lax.all_gather(coarse_rhs, 'space', axis=2, tiled=True)  7.42 us
    ppermute x4, waiting for transfers between devices, extended(): after = lax.ppermute(first, axis, down)  6.92 us
    unnamed x13, local copies, waits for them, and re-layouts  5.71 us
    ppermute x4, starting transfers between devices, extended(): after = lax.ppermute(first, axis, down)  5.57 us
  transfers between devices with their start and end apart: 9, of which 4 were waited for; matrix products, arithmetic and copies ran while one was open for 5% of the time, Pallas kernels for 0%

commit v1 on v0

v1 whole, which is shorter than its diff:
```python
import functools
import math

import jax
import jax.numpy as jnp
from jax import lax
from jax.experimental import pallas as pl
from jax.experimental.pallas import tpu as pltpu
from jax.sharding import PartitionSpec as P

HX = 128
HY = 8
T_STEPS = 64
COARSE_SWEEPS = 8
OMEGA = 0.7
MESH = pl.DeviceIdType.MESH
F32 = jnp.float32


def poles(nodes, node_count):
    angles = -math.pi + (nodes + 0.5) * (2.0 * math.pi / node_count)
    scale = 0.5 * node_count
    sine = jnp.sin(angles)
    cot = jnp.cos(angles) / sine
    pole_r = scale * (0.5017 * angles * cot - 0.4622)
    pole_i = scale * 0.2645 * angles
    slope_r = scale * 0.5017 * (cot - angles / (sine * sine))
    weight_r = scale * 0.2645 / node_count
    weight_i = -slope_r / node_count
    return pole_r, pole_i, weight_r, weight_i


def iota(shape, axis):
    return lax.broadcasted_iota(jnp.int32, shape, len(shape) + axis)


def shift(v, lanes, rows):
    if lanes:
        v = pltpu.roll(v, lanes % HX, v.ndim - 1)
    if rows:
        v = pltpu.roll(v, rows % HY, v.ndim - 2)
    return v


def sides(v, step):
    lane, row = iota(v.shape, -1), iota(v.shape, -2)
    left = jnp.where(lane >= step, shift(v, step, 0), 0.0)
    right = jnp.where(lane < HX - step, shift(v, -step, 0), 0.0)
    front = jnp.where(row >= step, shift(v, 0, step), 0.0)
    back = jnp.where(row < HY - step, shift(v, 0, -step), 0.0)
    return (left + right) + (front + back)


def even_lane(shape):
    return iota(shape, -1) % 2 == 0


def even_row(shape):
    return iota(shape, -2) % 2 == 0


def partner_lane(v):
    return jnp.where(even_lane(v.shape), shift(v, -1, 0), shift(v, 1, 0))


def partner_row(v):
    return jnp.where(even_row(v.shape), shift(v, 0, -1), shift(v, 0, 1))


def pack(a0, a1, a2, a3):
    el, er = even_lane(a0.shape), even_row(a0.shape)
    h0 = jnp.where(el, a0, a1) + jnp.where(el, shift(a0, -1, 0), shift(a1, 1, 0))
    h1 = jnp.where(el, a2, a3) + jnp.where(el, shift(a2, -1, 0), shift(a3, 1, 0))
    return jnp.where(er, h0, h1) + jnp.where(er, shift(h0, 0, -1), shift(h1, 0, 1))


def next_slot(v):
    return jnp.where(
        even_lane(v.shape),
        shift(v, -1, 0),
        jnp.where(even_row(v.shape), shift(v, 1, -1), 0.0),
    )


def last_slot(v):
    return jnp.where(
        even_lane(v.shape),
        jnp.where(even_row(v.shape), 0.0, shift(v, -1, 1)),
        shift(v, 1, 0),
    )


def prolong(v, slot):
    v = jnp.where(iota(v.shape, -1) % 2 == slot % 2, v, partner_lane(v))
    return jnp.where(iota(v.shape, -2) % 2 == slot // 2, v, partner_row(v))


def scaled(real, imag, v):
    re, im = v[:3], v[3:]
    return jnp.concatenate([real * re - imag * im, real * im + imag * re], axis=0)


def kernel(
    S, C, NS, L, D, NT, W,
    body_ref, thick_ref, mask_ref, layer_ref, shear_ref, relax_ref, node_ref, time_ref,
    field_ref, surf_ref,
    body_all, layer_all, tab, inv, coef, base, u1, u2, cnt, rz, coarse, top, sbuf, rbuf,
    body_send, body_recv, layer_send, layer_recv, surf_send, surf_recv,
):
    NZ = S * D
    NCZ = NZ // 2
    NJ = NCZ // 4
    NTP = sbuf.shape[2]
    R = sbuf.shape[0]
    tile = (HY, HX)
    me_s = lax.axis_index("space")
    me_c = lax.axis_index("contour")

    barrier = pltpu.get_barrier_semaphore()
    for k in range(1, S):
        pl.semaphore_signal(
            barrier, inc=1, device_id={"space": lax.rem(me_s + k, S)}, device_id_type=MESH
        )
    for k in range(1, C):
        pl.semaphore_signal(
            barrier, inc=1, device_id={"contour": lax.rem(me_c + k, C)}, device_id_type=MESH
        )
    pl.semaphore_wait(barrier, S + C - 2)

    def slab_copies(k):
        peer = {"space": lax.rem(me_s + k, S)}
        return (
            pltpu.make_async_remote_copy(
                layer_ref, layer_all.at[me_s], layer_send.at[k], layer_recv.at[k],
                device_id=peer, device_id_type=MESH,
            ),
            pltpu.make_async_remote_copy(
                body_ref, body_all.at[me_s], body_send.at[k], body_recv.at[k],
                device_id=peer, device_id_type=MESH,
            ),
        )

    sends = [slab_copies(k) for k in range(1, S)]
    for pair in sends:
        for copy in pair:
            copy.start()

    node_vec = jnp.stack([jnp.full(tile, node_ref[n].astype(F32)) for n in range(NS)])
    pole_r, pole_i, weight_r, weight_i = poles(node_vec, NS * C)
    square = pole_r * pole_r + pole_i * pole_i
    inv_r, inv_i = pole_r / square, -pole_i / square
    for n in range(NS):
        inv[n, 0] = inv_r[n]
        inv[n, 1] = inv_i[n]
    for l in range(L):
        shear, relax = shear_ref[l], relax_ref[l]
        moved = pole_r + relax
        denom = moved * moved + pole_i * pole_i
        mu_r = shear * ((pole_r * moved + pole_i * pole_i) / denom)
        mu_i = shear * ((pole_i * moved - pole_r * pole_i) / denom)
        size = shear * jnp.sqrt(square / denom)
        diag_r, diag_i = 6.0 * mu_r + 1.0, 6.0 * mu_i
        bound = 6.0 * size + 1.0
        scale = OMEGA / (bound * bound)
        gain_r, gain_i = diag_r * scale, -diag_i * scale
        rows = (
            1.0 - scale * (diag_r * diag_r + diag_i * diag_i),
            gain_r * mu_r - gain_i * mu_i,
            gain_r * mu_i + gain_i * mu_r,
            gain_r * inv_r - gain_i * inv_i,
            gain_r * inv_i + gain_i * inv_r,
            mu_r,
            mu_i,
            size,
        )
        for q, value in enumerate(rows):
            for n in range(NS):
                tab[n, l, q] = value[n]

    spots = iota((NTP, HX), -2)
    times = jnp.zeros((NTP, HX), F32)
    for j in range(NT):
        times = jnp.where(spots == j, (time_ref[j].astype(F32) + 1.0) * (2.0 / T_STEPS), times)
    factors = []
    for n in range(NS):
        growth = jnp.exp(times * pole_r[n, :1, :])
        phase = times * pole_i[n, :1, :]
        cosine, sine = jnp.cos(phase), jnp.sin(phase)
        wi = weight_i[n, :1, :]
        factors.append(
            (growth * (weight_r * cosine - wi * sine), growth * (weight_r * sine + wi * cosine))
        )

    blank = jnp.zeros((NS, 2, 6) + tile, F32)
    for u in (u1, u2):
        u[:, pl.ds(0, 2)] = blank
        u[:, pl.ds(NZ + 2, 2)] = blank

    body_all[me_s] = body_ref[...]
    layer_all[me_s] = layer_ref[...]
    ice = thick_ref[...] * mask_ref[...].astype(F32)

    def take_slab(slab):
        for zp in range(D // 2):
            counts = None
            for z in (2 * zp, 2 * zp + 1):
                at = slab * D + z
                ids = layer_all[slab, pl.ds(z, HY, stride=D), :]
                force = jnp.stack(
                    [body_all[slab, c, pl.ds(z, HY, stride=D), :] for c in range(3)]
                )
                if z == 0:
                    load = jnp.where(slab == 0, ice, jnp.zeros_like(ice))
                    force = jnp.concatenate([(force[0] - load)[None], force[1:]], axis=0)
                base[at] = force
                one = [jnp.where(ids == l, 1.0, 0.0) for l in range(1, L)]
                counts = one if counts is None else [a + b for a, b in zip(counts, one)]
                wide = jnp.broadcast_to(ids[None], (7,) + tile)
                for n in range(NS):
                    value = tab[n, 0, pl.ds(0, 7)]
                    for l in range(1, L):
                        value = jnp.where(wide == l, tab[n, l, pl.ds(0, 7)], value)
                    coef[n, at] = value
                    u1[n, at + 2] = jnp.concatenate(
                        [value[3][None] * force, value[4][None] * force], axis=0
                    )
            for l in range(L - 1):
                cnt[slab * (D // 2) + zp, l] = counts[l]

    take_slab(me_s)

    def arrive(k, carry):
        for copy in slab_copies(k):
            copy.wait_recv()
        take_slab(lax.rem(me_s - k + S, S))
        return carry

    lax.fori_loop(1, S, arrive, 0)

    def sweep(n, at, v, below, above):
        co = coef[n, at]
        around = below + above + sides(v, 1)
        return u1[n, at + 2] + co[0][None] * v + scaled(co[1][None], co[2][None], around)

    def second(i, carry):
        n, z = i // NZ, i % NZ
        u2[n, z + 2] = sweep(n, z, u1[n, z + 2], u1[n, z + 1], u1[n, z + 3])
        return carry

    lax.fori_loop(0, NS * NZ, second, 0, unroll=2)

    def residual(i, carry):
        n, zc = i // NCZ, i % NCZ
        total = None
        for z in (2 * zc, 2 * zc + 1):
            mu_r, mu_i = coef[n, z, 5][None], coef[n, z, 6][None]
            force = base[z]
            v = u2[n, z + 2]
            lap = u2[n, z + 1] + u2[n, z + 3] + sides(v, 1) - 6.0 * v
            right = jnp.concatenate([inv[n, 0][None] * force, inv[n, 1][None] * force], axis=0)
            r = right - v + scaled(mu_r, mu_i, lap)
            total = r if total is None else total + r
        rz[n, zc] = total
        return carry

    lax.fori_loop(0, NS * NCZ, residual, 0)

    counts = [pack(*[cnt[q * NJ + j] for q in range(4)]) * 0.125 for j in range(NJ)]

    def solve(n, carry):
        rhs, first, dd, hr, hi, mr, mi = [], [], [], [], [], [], []
        for j in range(NJ):
            share = [counts[j][l] for l in range(L - 1)]
            rest = 1.0 - sum(share[1:], share[0])
            mixed = []
            for q in (5, 6, 7):
                value = rest * tab[n, 0, q]
                for l in range(1, L):
                    value = value + share[l - 1] * tab[n, l, q]
                mixed.append(value)
            mu_r, mu_i, size = mixed
            diag_r, diag_i = 1.5 * mu_r + 1.0, 1.5 * mu_i
            bound = 1.5 * size + 1.0
            scale = OMEGA / (bound * bound)
            gain_r, gain_i = diag_r * scale, -diag_i * scale
            mu_r, mu_i = 0.25 * mu_r, 0.25 * mu_i
            b = pack(*[rz[n, q * NJ + j] for q in range(4)]) * 0.125
            rhs.append(b)
            first.append(scaled(gain_r[None], gain_i[None], b))
            dd.append((1.0 - scale * (diag_r * diag_r + diag_i * diag_i))[None])
            hr.append((gain_r * mu_r - gain_i * mu_i)[None])
            hi.append((gain_r * mu_i + gain_i * mu_r)[None])
            mr.append(mu_r[None])
            mi.append(mu_i[None])

        def around(e):
            out = []
            for j in range(NJ):
                above = e[j + 1] if j < NJ - 1 else next_slot(e[0])
                below = e[j - 1] if j > 0 else last_slot(e[NJ - 1])
                out.append(above + below + sides(e[j], 2))
            return out

        def step(counter, e):
            near = around(e)
            return tuple(
                first[j] + dd[j] * e[j] + scaled(hr[j], hi[j], near[j]) for j in range(NJ)
            )

        e = lax.fori_loop(0, COARSE_SWEEPS - 1, step, tuple(first))
        near = around(e)
        left = None
        for j in range(NJ):
            part = rhs[j] - e[j] + scaled(mr[j], mi[j], near[j] - 6.0 * e[j])
            left = part if left is None else left + part
        left = left + partner_lane(left)
        left = (left + partner_row(left)) * (1.0 / NCZ)
        for j in range(NJ):
            coarse[n, j] = e[j] + left
        return carry

    lax.fori_loop(0, NS, solve, 0)

    def window(n, start, reach_up, count):
        lo = -2 if reach_up else 0
        third = {}
        for z in range(lo, count + 2, 2):
            zc = start // 2 + z // 2
            inside = jnp.where((zc >= 0) & (zc < NCZ), 1.0, 0.0)
            at = jnp.clip(zc, 0, NCZ - 1)
            e = prolong(coarse[n, at % NJ], at // NJ) * inside
            for zz in (z, z + 1):
                if zz < count + 2:
                    third[zz] = u2[n, start + zz + 2] + e
        zero = jnp.zeros((6,) + tile, F32)
        fourth = {}
        for z in range(max(lo + 1, lo if reach_up else 0) if reach_up else 0, count + 1):
            at = start + z
            inside = jnp.where((at >= 0) & (at < NZ), 1.0, 0.0)
            value = sweep(n, jnp.clip(at, 0, NZ - 1), third[z], third.get(z - 1, zero), third[z + 1])
            fourth[z] = value * inside
        return [
            sweep(n, start + z, fourth[z], fourth.get(z - 1, zero), fourth[z + 1])
            for z in range(count)
        ]

    def surface(n, carry):
        top[n] = window(n, jnp.int32(0), False, 1)[0]
        return carry

    lax.fori_loop(0, NS, surface, 0)

    row0 = (me_s * (C * W)) // HX
    for r in range(R):
        for c in range(3):
            total = None
            for n in range(NS):
                re = top[n, c, pl.ds(row0 + r, 1), :]
                im = top[n, c + 3, pl.ds(row0 + r, 1), :]
                part = factors[n][0] * re - factors[n][1] * im
                total = part if total is None else total + part
            sbuf[r, c] = total

    def surf_copy(k):
        to = lax.rem(me_c + k, C)
        return pltpu.make_async_remote_copy(
            sbuf.at[(to * W) // HX if R > 1 else 0], rbuf.at[k - 1],
            surf_send.at[k], surf_recv.at[k],
            device_id={"contour": to}, device_id_type=MESH,
        )

    surf_sends = [surf_copy(k) for k in range(1, C)]
    for copy in surf_sends:
        copy.start()

    def finish(n, carry):
        for z, value in enumerate(window(n, me_s * D, True, D)):
            for c in range(6):
                field_ref[n, c, pl.ds(z, HY, stride=D), :] = value[c]
        return carry

    lax.fori_loop(0, NS, finish, 0)

    for copy in surf_sends:
        copy.wait_recv()
    total = sbuf[(me_c * W) // HX if R > 1 else 0]
    for k in range(1, C):
        total = total + rbuf[k - 1]
    offset = lax.rem((me_s * C + me_c) * W, HX)
    surf_ref[...] = pltpu.roll(total, lax.rem(HX - offset, HX), 2)

    for copy in surf_sends:
        copy.wait_send()
    for pair in sends:
        for copy in pair:
            copy.wait_send()


def per_device(
    body_force, ice_thickness, ice_mask, layer_ids, shear_modulus, relax_rate, node_ids, time_ids
):
    S, C = lax.axis_size("space"), lax.axis_size("contour")
    NS, L, D, NT = node_ids.shape[0], shear_modulus.shape[0], layer_ids.shape[0], time_ids.shape[0]
    NZ = S * D
    NCZ = NZ // 2
    NJ = NCZ // 4
    W = HX * HY // (S * C)
    R = max(1, C * W // HX)
    NTP = -(-NT // 8) * 8
    body = body_force.reshape(3, D, HY, HX).transpose(0, 2, 1, 3).reshape(3, HY * D, HX)
    layers = layer_ids.reshape(D, HY, HX).transpose(1, 0, 2).reshape(HY * D, HX)
    tile = (HY, HX)
    vmem = pl.BlockSpec(memory_space=pltpu.VMEM)
    smem = pl.BlockSpec(memory_space=pltpu.SMEM)
    field, surf = pl.pallas_call(
        functools.partial(kernel, S, C, NS, L, D, NT, W),
        out_shape=(
            jax.ShapeDtypeStruct((NS, 6, HY * D, HX), F32),
            jax.ShapeDtypeStruct((3, NTP, HX), F32),
        ),
        in_specs=[vmem] * 4 + [smem] * 4,
        out_specs=(vmem, vmem),
        scratch_shapes=[
            pltpu.VMEM((S, 3, HY * D, HX), F32),
            pltpu.VMEM((S, HY * D, HX), jnp.int32),
            pltpu.VMEM((NS, L, 8) + tile, F32),
            pltpu.VMEM((NS, 2) + tile, F32),
            pltpu.VMEM((NS, NZ, 7) + tile, F32),
            pltpu.VMEM((NZ, 3) + tile, F32),
            pltpu.VMEM((NS, NZ + 4, 6) + tile, F32),
            pltpu.VMEM((NS, NZ + 4, 6) + tile, F32),
            pltpu.VMEM((NCZ, L - 1) + tile, F32),
            pltpu.VMEM((NS, NCZ, 6) + tile, F32),
            pltpu.VMEM((NS, NJ, 6) + tile, F32),
            pltpu.VMEM((NS, 6) + tile, F32),
            pltpu.VMEM((R, 3, NTP, HX), F32),
            pltpu.VMEM((C - 1, 3, NTP, HX), F32),
            pltpu.SemaphoreType.DMA((S,)),
            pltpu.SemaphoreType.DMA((S,)),
            pltpu.SemaphoreType.DMA((S,)),
            pltpu.SemaphoreType.DMA((S,)),
            pltpu.SemaphoreType.DMA((C,)),
            pltpu.SemaphoreType.DMA((C,)),
        ],
        compiler_params=pltpu.CompilerParams(
            collective_id=0, has_side_effects=True, vmem_limit_bytes=48 * 1024 * 1024
        ),
    )(
        body,
        ice_thickness.reshape(HY, HX),
        ice_mask.reshape(HY, HX),
        layers,
        shear_modulus,
        relax_rate,
        node_ids,
        time_ids,
    )
    field = field.reshape(NS, 6, HY, D, HX).transpose(0, 1, 3, 2, 4).reshape(NS, 6, D, HY * HX)
    surf = surf[:, :NT, :W].transpose(1, 0, 2)
    return (field, surf)


def solution(mesh):
    in_specs = (
        P("groups", "space", None),
        P("groups"),
        P("groups"),
        P("space", None),
        P(),
        P(),
        P("contour"),
        P("groups"),
    )
    out_specs = (
        P(("groups", "contour"), None, "space", None),
        P("groups", None, ("space", "contour")),
    )
    return jax.shard_map(
        per_device, mesh=mesh, in_specs=in_specs, out_specs=out_specs, check_vma=False
    )
```

time: 153 us -> 28.6 us (0.19)
  waiting for transfers between devices: 64.7 us -> 0 us
  Pallas kernels: 0 us -> 23.4 us
  local copies, waits for them, and re-layouts: 26.7 us -> 4.21 us
  starting transfers between devices: 17.4 us -> 0 us
  blocking collectives: 15.6 us -> 0 us
  between operations: 15.1 us -> 0.69 us
  other arithmetic: 12.1 us -> 0 us
    unnamed x2 -> x0, waiting for transfers between devices: 57.8 us -> none
    pallas_call x0 -> x1, Pallas kernels: none -> 23.4 us  [per_device(): pl.pallas_call(functools.partial(kernel, S, C, NS, L, D, NT, W), out_shap...]
    slice x32 -> x0, local copies, waits for them, and re-layouts: 18.7 us -> none  [the longest x8 16 us: restrict(): column_pairs = values[..., 0::2] + values[..., 1::2]]
    ppermute x8 -> x0, starting transfers between devices: 17.4 us -> none  [the longest x4 11.8 us: extended(): before = lax.ppermute(last, axis, up)]
    all_gather x2 -> x0, blocking collectives: 15.6 us -> none  [the longest x1 8.21 us: per_device(): lax.all_gather(stacked, 'space', axis=2, tiled=True)]
    ppermute x8 -> x0, waiting for transfers between devices: 6.93 us -> none  [the longest x4 6.92 us: extended(): after = lax.ppermute(first, axis, down)]
    sub x27 -> x0, other arithmetic: 3.32 us -> none  [the longest x4 1.79 us: operate(): 6.0 * center - padded[..., :-2, :] - padded[..., 2:, :]]
    mul x16 -> x0, other arithmetic: 2.8 us -> none  [the longest x8 1.21 us: operate(): (6.0 * center - padded[..., :-2, :] - padded[..., 2:, :] - horizontal(cen...]
  transfers between devices with their start and end apart: 9 -> 0, of which waited for: 4 -> 0; matrix products, arithmetic and copies ran while one was open for 5% -> 0% of each run, Pallas kernels for 0% -> 0%
where the time goes in v1:
time: 28.6 us; the launch traced here: 28.3 us
  Pallas kernels  23.4 us (82%)
  local copies, waits for them, and re-layouts  4.21 us (15%)
  between operations  0.69 us (2%)
    pallas_call x1, Pallas kernels, per_device(): pl.pallas_call(functools.partial(kernel, S, C, NS, L, D, NT, W), out_shap...  23.4 us
    unnamed x18, local copies, waits for them, and re-layouts  4.21 us

profile of v1, /device:TPU:0, one launch (start us, length us, event | category | flops | bytes accessed | tf_op | source)
XLA Modules:
  0.0 28.3 jit_solution(7116059219694256004)
XLA Ops:
  0.6 0.0 copy-start.2
  0.6 0.0 copy-start.7
  0.7 0.0 copy-start.4
  0.7 0.0 copy-start.5
  0.7 0.0 copy-start.6
  0.7 0.6 %copy-done.2 = f32[1024]{0:T(1024)S(1)} copy-done((f32[1024]{0:T(1024)S(1)}, f32[1024]{0:T(1024)}, u32[]{:S(2)}) %copy-start.2) | copy-done | bytes 4120
  1.3 0.0 copy-done.7
  1.3 0.0 copy-done.4
  1.3 0.0 copy-done.5
  1.3 0.0 copy-done.6
  1.4 0.0 copy-start
  1.4 0.8 %copy-done = f32[3,4,1024]{2,1,0:T(4,128)S(1)} copy-done((f32[3,4,1024]{2,1,0:T(4,128)S(1)}, f32[3,4,1024]{2,1,0:T(4,128)}, u32[]{:S(2)}) %copy-start) | copy-done | bytes 49176
  2.2 0.0 copy-start.1
  2.2 0.7 %copy-done.1 = s32[4,1024]{1,0:T(4,128)S(1)} copy-done((s32[4,1024]{1,0:T(4,128)S(1)}, s32[4,1024]{1,0:T(4,128)}, u32[]{:S(2)}) %copy-start.1) | copy-done | bytes 16408
  2.9 0.0 copy-start.3
  2.9 0.7 %copy-done.3 = s32[1024]{0:T(1024)S(1)} copy-done((s32[1024]{0:T(1024)S(1)}, s32[1024]{0:T(1024)}, u32[]{:S(2)}) %copy-start.3) | copy-done | bytes 4120
  3.6 23.4 %shard_map.95 = (f32[3,6,32,128]{3,2,1,0:T(8,128)S(1)}, f32[3,16,128]{2,1,0:T(8,128)S(1)}) custom-call(f32[3,32,128]{2,1,0:T(8,128)S(1)} %bitcast.20, f32[8,128]{1,0:T(8,128)S(1)} %bitcast.22, s32[8,128]{1,0:T(8,128)S(1)} %bitcast.23, s32[32,128]{1,0:T(8,128)S(1)} %bitcast.21, f32[4]{0:T(128)S(1)} %copy-done.4, f32[4]{0:T(128)S(1)} %copy-done.5, ...), custom_call_target="tpu_custom_call" | custom-call | tf_op jit(solution)/shard_map/pallas_call | solution.py:415
  26.9 0.6 %copy.13 = f32[12,3,64]{2,1,0:T(4,128)} copy(f32[12,3,64]{2,0,1:T(8,128)S(1)} %slice_bitcast_fusion) | data formatting | bytes 18432
  27.6 0.7 %copy.15 = f32[3,6,4,1024]{3,2,1,0:T(4,128)} copy(f32[3,6,4,1024]{3,2,1,0:T(4,128)S(1)} %bitcast.19) | data formatting | bytes 589824
  (1 shorter events, 0.0 us)
Async XLA Ops:
  0.6 0.7 %copy-start.2 = (f32[1024]{0:T(1024)S(1)}, f32[1024]{0:T(1024)}, u32[]{:S(2)}) copy-start(f32[1024]{0:T(1024)} %param.9) | copy-start | bytes 12292
  0.6 0.7 %copy-start.7 = (s32[12]{0:T(128)S(1)}, s32[12]{0:T(128)}, u32[]{:S(2)}) copy-start(s32[12]{0:T(128)} %time_ref.1) | copy-start | bytes 148
  0.7 0.7 %copy-start.4 = (f32[4]{0:T(128)S(1)}, f32[4]{0:T(128)}, u32[]{:S(2)}) copy-start(f32[4]{0:T(128)} %shear_ref.1) | copy-start | bytes 52
  0.7 0.7 %copy-start.5 = (f32[4]{0:T(128)S(1)}, f32[4]{0:T(128)}, u32[]{:S(2)}) copy-start(f32[4]{0:T(128)} %relax_ref.1) | copy-start | bytes 52
  0.7 0.7 %copy-start.6 = (s32[3]{0:T(128)S(1)}, s32[3]{0:T(128)}, u32[]{:S(2)}) copy-start(s32[3]{0:T(128)} %node_ref.1) | copy-start | bytes 40
  1.4 0.8 %copy-start = (f32[3,4,1024]{2,1,0:T(4,128)S(1)}, f32[3,4,1024]{2,1,0:T(4,128)}, u32[]{:S(2)}) copy-start(f32[3,4,1024]{2,1,0:T(4,128)} %param.8) | copy-start | bytes 147460
  2.2 0.7 %copy-start.1 = (s32[4,1024]{1,0:T(4,128)S(1)}, s32[4,1024]{1,0:T(4,128)}, u32[]{:S(2)}) copy-start(s32[4,1024]{1,0:T(4,128)} %param.11) | copy-start | bytes 49156
  2.9 0.7 %copy-start.3 = (s32[1024]{0:T(1024)S(1)}, s32[1024]{0:T(1024)}, u32[]{:S(2)}) copy-start(s32[1024]{0:T(1024)} %param.10) | copy-start | bytes 12292

commit v2 on v1

--- a/solution.py
+++ b/solution.py
@@ -102,8 +102,9 @@
 
 def kernel(
     S, C, NS, L, D, NT, W,
-    body_ref, thick_ref, mask_ref, layer_ref, shear_ref, relax_ref, node_ref, time_ref,
+    body_in, thick_in, mask_in, layer_in, shear_in, relax_in, node_in, time_in,
     field_ref, surf_ref,
+    thick_ref, mask_ref, shear_ref, relax_ref, node_ref, time_ref, load_sem,
     body_all, layer_all, tab, inv, coef, base, u1, u2, cnt, rz, coarse, top, sbuf, rbuf,
     body_send, body_recv, layer_send, layer_recv, surf_send, surf_recv,
 ):
@@ -125,17 +126,36 @@
         pl.semaphore_signal(
             barrier, inc=1, device_id={"contour": lax.rem(me_c + k, C)}, device_id_type=MESH
         )
+    loads = [
+        pltpu.make_async_copy(source, target, load_sem.at[i])
+        for i, (source, target) in enumerate(
+            (
+                (layer_in, layer_all.at[me_s]),
+                (body_in, body_all.at[me_s]),
+                (node_in, node_ref),
+                (shear_in, shear_ref),
+                (relax_in, relax_ref),
+                (time_in, time_ref),
+                (thick_in, thick_ref),
+                (mask_in, mask_ref),
+            )
+        )
+    ]
+    for copy in loads:
+        copy.start()
+    for copy in loads:
+        copy.wait()
     pl.semaphore_wait(barrier, S + C - 2)
 
     def slab_copies(k):
         peer = {"space": lax.rem(me_s + k, S)}
         return (
             pltpu.make_async_remote_copy(
-                layer_ref, layer_all.at[me_s], layer_send.at[k], layer_recv.at[k],
+                layer_all.at[me_s], layer_all.at[me_s], layer_send.at[k], layer_recv.at[k],
                 device_id=peer, device_id_type=MESH,
             ),
             pltpu.make_async_remote_copy(
-                body_ref, body_all.at[me_s], body_send.at[k], body_recv.at[k],
+                body_all.at[me_s], body_all.at[me_s], body_send.at[k], body_recv.at[k],
                 device_id=peer, device_id_type=MESH,
             ),
         )
@@ -196,8 +216,6 @@
         u[:, pl.ds(0, 2)] = blank
         u[:, pl.ds(NZ + 2, 2)] = blank
 
-    body_all[me_s] = body_ref[...]
-    layer_all[me_s] = layer_ref[...]
     ice = thick_ref[...] * mask_ref[...].astype(F32)
 
     def take_slab(slab):
@@ -242,32 +260,32 @@
         around = below + above + sides(v, 1)
         return u1[n, at + 2] + co[0][None] * v + scaled(co[1][None], co[2][None], around)
 
-    def second(i, carry):
-        n, z = i // NZ, i % NZ
-        u2[n, z + 2] = sweep(n, z, u1[n, z + 2], u1[n, z + 1], u1[n, z + 3])
+    def second(z, carry):
+        for n in range(NS):
+            u2[n, z + 2] = sweep(n, z, u1[n, z + 2], u1[n, z + 1], u1[n, z + 3])
         return carry
 
-    lax.fori_loop(0, NS * NZ, second, 0, unroll=2)
-
-    def residual(i, carry):
-        n, zc = i // NCZ, i % NCZ
-        total = None
-        for z in (2 * zc, 2 * zc + 1):
-            mu_r, mu_i = coef[n, z, 5][None], coef[n, z, 6][None]
-            force = base[z]
-            v = u2[n, z + 2]
-            lap = u2[n, z + 1] + u2[n, z + 3] + sides(v, 1) - 6.0 * v
-            right = jnp.concatenate([inv[n, 0][None] * force, inv[n, 1][None] * force], axis=0)
-            r = right - v + scaled(mu_r, mu_i, lap)
-            total = r if total is None else total + r
-        rz[n, zc] = total
+    lax.fori_loop(0, NZ, second, 0, unroll=4)
+
+    def residual(zc, carry):
+        for n in range(NS):
+            total = None
+            for z in (2 * zc, 2 * zc + 1):
+                mu_r, mu_i = coef[n, z, 5][None], coef[n, z, 6][None]
+                force = base[z]
+                v = u2[n, z + 2]
+                lap = u2[n, z + 1] + u2[n, z + 3] + sides(v, 1) - 6.0 * v
+                right = jnp.concatenate([inv[n, 0][None] * force, inv[n, 1][None] * force], axis=0)
+                r = right - v + scaled(mu_r, mu_i, lap)
+                total = r if total is None else total + r
+            rz[n, zc] = total
         return carry
 
-    lax.fori_loop(0, NS * NCZ, residual, 0)
+    lax.fori_loop(0, NCZ, residual, 0, unroll=2)
 
     counts = [pack(*[cnt[q * NJ + j] for q in range(4)]) * 0.125 for j in range(NJ)]
 
-    def solve(n, carry):
+    def prepare(n):
         rhs, first, dd, hr, hi, mr, mi = [], [], [], [], [], [], []
         for j in range(NJ):
             share = [counts[j][l] for l in range(L - 1)]
@@ -292,22 +310,35 @@
             hi.append((gain_r * mu_i + gain_i * mu_r)[None])
             mr.append(mu_r[None])
             mi.append(mu_i[None])
-
-        def around(e):
-            out = []
-            for j in range(NJ):
-                above = e[j + 1] if j < NJ - 1 else next_slot(e[0])
-                below = e[j - 1] if j > 0 else last_slot(e[NJ - 1])
-                out.append(above + below + sides(e[j], 2))
-            return out
-
-        def step(counter, e):
+        return rhs, first, dd, hr, hi, mr, mi
+
+    def around(e):
+        out = []
+        for j in range(NJ):
+            above = e[j + 1] if j < NJ - 1 else next_slot(e[0])
+            below = e[j - 1] if j > 0 else last_slot(e[NJ - 1])
+            out.append(above + below + sides(e[j], 2))
+        return out
+
+    plans = [prepare(n) for n in range(NS)]
+
+    def step(counter, states):
+        new = []
+        for n in range(NS):
+            rhs, first, dd, hr, hi, mr, mi = plans[n]
+            e = states[n]
             near = around(e)
-            return tuple(
-                first[j] + dd[j] * e[j] + scaled(hr[j], hi[j], near[j]) for j in range(NJ)
+            new.append(
+                tuple(first[j] + dd[j] * e[j] + scaled(hr[j], hi[j], near[j]) for j in range(NJ))
             )
-
-        e = lax.fori_loop(0, COARSE_SWEEPS - 1, step, tuple(first))
+        return tuple(new)
+
+    states = lax.fori_loop(
+        0, COARSE_SWEEPS - 1, step, tuple(tuple(plans[n][1]) for n in range(NS))
+    )
+    for n in range(NS):
+        rhs, first, dd, hr, hi, mr, mi = plans[n]
+        e = states[n]
         near = around(e)
         left = None
         for j in range(NJ):
@@ -317,9 +348,6 @@
         left = (left + partner_row(left)) * (1.0 / NCZ)
         for j in range(NJ):
             coarse[n, j] = e[j] + left
-        return carry
-
-    lax.fori_loop(0, NS, solve, 0)
 
     def window(n, start, reach_up, count):
         lo = -2 if reach_up else 0
@@ -344,11 +372,8 @@
             for z in range(count)
         ]
 
-    def surface(n, carry):
+    for n in range(NS):
         top[n] = window(n, jnp.int32(0), False, 1)[0]
-        return carry
-
-    lax.fori_loop(0, NS, surface, 0)
 
     row0 = (me_s * (C * W)) // HX
     for r in range(R):
@@ -411,16 +436,22 @@
     layers = layer_ids.reshape(D, HY, HX).transpose(1, 0, 2).reshape(HY * D, HX)
     tile = (HY, HX)
     vmem = pl.BlockSpec(memory_space=pltpu.VMEM)
-    smem = pl.BlockSpec(memory_space=pltpu.SMEM)
     field, surf = pl.pallas_call(
         functools.partial(kernel, S, C, NS, L, D, NT, W),
         out_shape=(
             jax.ShapeDtypeStruct((NS, 6, HY * D, HX), F32),
             jax.ShapeDtypeStruct((3, NTP, HX), F32),
         ),
-        in_specs=[vmem] * 4 + [smem] * 4,
+        in_specs=[pl.BlockSpec(memory_space=pltpu.HBM)] * 8,
         out_specs=(vmem, vmem),
         scratch_shapes=[
+            pltpu.VMEM(tile, F32),
+            pltpu.VMEM(tile, jnp.int32),
+            pltpu.SMEM((L,), F32),
+            pltpu.SMEM((L,), F32),
+            pltpu.SMEM((NS,), jnp.int32),
+            pltpu.SMEM((NT,), jnp.int32),
+            pltpu.SemaphoreType.DMA((8,)),
             pltpu.VMEM((S, 3, HY * D, HX), F32),
             pltpu.VMEM((S, HY * D, HX), jnp.int32),
             pltpu.VMEM((NS, L, 8) + tile, F32),

time: 28.6 us -> 22.8 us (0.80)
  Pallas kernels: 23.4 us -> 17.6 us
    pallas_call x1, Pallas kernels: 23.4 us -> 17.6 us  [per_device(): pl.pallas_call(functools.partial(kernel, S, C, NS, L, D, NT, W), out_shap...]
where the time goes in v2:
time: 22.8 us; the launch traced here: 22.5 us
  Pallas kernels  17.6 us (77%)
  local copies, waits for them, and re-layouts  4.21 us (18%)
  between operations  0.69 us (3%)
    pallas_call x1, Pallas kernels, per_device(): pl.pallas_call(functools.partial(kernel, S, C, NS, L, D, NT, W), out_shap...  17.6 us
    unnamed x18, local copies, waits for them, and re-layouts  4.21 us

profile of v2, /device:TPU:0, one launch (start us, length us, event | category | flops | bytes accessed | tf_op | source)
XLA Modules:
  0.0 22.5 jit_solution(14406857024021412018)
XLA Ops:
  0.6 0.0 copy-start.2
  0.6 0.0 copy-start.7
  0.7 0.0 copy-start.4
  0.7 0.0 copy-start.5
  0.7 0.0 copy-start.6
  0.7 0.6 %copy-done.2 = f32[1024]{0:T(1024)S(1)} copy-done((f32[1024]{0:T(1024)S(1)}, f32[1024]{0:T(1024)}, u32[]{:S(2)}) %copy-start.2) | copy-done | bytes 4120
  1.3 0.0 copy-done.7
  1.3 0.0 copy-done.4
  1.3 0.0 copy-done.5
  1.3 0.0 copy-done.6
  1.4 0.0 copy-start
  1.4 0.8 %copy-done = f32[3,4,1024]{2,1,0:T(4,128)S(1)} copy-done((f32[3,4,1024]{2,1,0:T(4,128)S(1)}, f32[3,4,1024]{2,1,0:T(4,128)}, u32[]{:S(2)}) %copy-start) | copy-done | bytes 49176
  2.2 0.0 copy-start.1
  2.2 0.7 %copy-done.1 = s32[4,1024]{1,0:T(4,128)S(1)} copy-done((s32[4,1024]{1,0:T(4,128)S(1)}, s32[4,1024]{1,0:T(4,128)}, u32[]{:S(2)}) %copy-start.1) | copy-done | bytes 16408
  2.9 0.0 copy-start.3
  2.9 0.7 %copy-done.3 = s32[1024]{0:T(1024)S(1)} copy-done((s32[1024]{0:T(1024)S(1)}, s32[1024]{0:T(1024)}, u32[]{:S(2)}) %copy-start.3) | copy-done | bytes 4120
  3.6 17.6 %shard_map.95 = (f32[3,6,32,128]{3,2,1,0:T(8,128)S(1)}, f32[3,16,128]{2,1,0:T(8,128)S(1)}) custom-call(f32[3,32,128]{2,1,0:T(8,128)S(1)} %bitcast.20, f32[8,128]{1,0:T(8,128)S(1)} %bitcast.22, s32[8,128]{1,0:T(8,128)S(1)} %bitcast.23, s32[32,128]{1,0:T(8,128)S(1)} %bitcast.21, f32[4]{0:T(128)S(1)} %copy-done.4, f32[4]{0:T(128)S(1)} %copy-done.5, ...), custom_call_target="tpu_custom_call" | custom-call | tf_op jit(solution)/shard_map/pallas_call | solution.py:439
  21.2 0.6 %copy.13 = f32[12,3,64]{2,1,0:T(4,128)} copy(f32[12,3,64]{2,0,1:T(8,128)S(1)} %slice_bitcast_fusion) | data formatting | bytes 18432
  21.8 0.7 %copy.15 = f32[3,6,4,1024]{3,2,1,0:T(4,128)} copy(f32[3,6,4,1024]{3,2,1,0:T(4,128)S(1)} %bitcast.19) | data formatting | bytes 589824
  (1 shorter events, 0.0 us)
Async XLA Ops:
  0.6 0.7 %copy-start.2 = (f32[1024]{0:T(1024)S(1)}, f32[1024]{0:T(1024)}, u32[]{:S(2)}) copy-start(f32[1024]{0:T(1024)} %param.9) | copy-start | bytes 12292
  0.6 0.7 %copy-start.7 = (s32[12]{0:T(128)S(1)}, s32[12]{0:T(128)}, u32[]{:S(2)}) copy-start(s32[12]{0:T(128)} %time_in.1) | copy-start | bytes 148
  0.7 0.7 %copy-start.4 = (f32[4]{0:T(128)S(1)}, f32[4]{0:T(128)}, u32[]{:S(2)}) copy-start(f32[4]{0:T(128)} %shear_in.1) | copy-start | bytes 52
  0.7 0.7 %copy-start.5 = (f32[4]{0:T(128)S(1)}, f32[4]{0:T(128)}, u32[]{:S(2)}) copy-start(f32[4]{0:T(128)} %relax_in.1) | copy-start | bytes 52
  0.7 0.7 %copy-start.6 = (s32[3]{0:T(128)S(1)}, s32[3]{0:T(128)}, u32[]{:S(2)}) copy-start(s32[3]{0:T(128)} %node_in.1) | copy-start | bytes 40
  1.4 0.8 %copy-start = (f32[3,4,1024]{2,1,0:T(4,128)S(1)}, f32[3,4,1024]{2,1,0:T(4,128)}, u32[]{:S(2)}) copy-start(f32[3,4,1024]{2,1,0:T(4,128)} %param.8) | copy-start | bytes 147460
  2.2 0.7 %copy-start.1 = (s32[4,1024]{1,0:T(4,128)S(1)}, s32[4,1024]{1,0:T(4,128)}, u32[]{:S(2)}) copy-start(s32[4,1024]{1,0:T(4,128)} %param.11) | copy-start | bytes 49156
  2.9 0.7 %copy-start.3 = (s32[1024]{0:T(1024)S(1)}, s32[1024]{0:T(1024)}, u32[]{:S(2)}) copy-start(s32[1024]{0:T(1024)} %param.10) | copy-start | bytes 12292

commit v3 on v2

--- a/solution.py
+++ b/solution.py
@@ -103,8 +103,8 @@
 def kernel(
     S, C, NS, L, D, NT, W,
     body_in, thick_in, mask_in, layer_in, shear_in, relax_in, node_in, time_in,
-    field_ref, surf_ref,
-    thick_ref, mask_ref, shear_ref, relax_ref, node_ref, time_ref, load_sem,
+    field_out, surf_ref,
+    field_ref, field_sem, thick_ref, mask_ref, shear_ref, relax_ref, node_ref, time_ref, load_sem,
     body_all, layer_all, tab, inv, coef, base, u1, u2, cnt, rz, coarse, top, sbuf, rbuf,
     body_send, body_recv, layer_send, layer_recv, surf_send, surf_recv,
 ):
@@ -143,7 +143,7 @@
     ]
     for copy in loads:
         copy.start()
-    for copy in loads:
+    for copy in loads[:2]:
         copy.wait()
     pl.semaphore_wait(barrier, S + C - 2)
 
@@ -164,6 +164,9 @@
     for pair in sends:
         for copy in pair:
             copy.start()
+
+    for copy in loads[2:]:
+        copy.wait()
 
     node_vec = jnp.stack([jnp.full(tile, node_ref[n].astype(F32)) for n in range(NS)])
     pole_r, pole_i, weight_r, weight_i = poles(node_vec, NS * C)
@@ -398,10 +401,14 @@
     for copy in surf_sends:
         copy.start()
 
+    def field_copy(n):
+        return pltpu.make_async_copy(field_ref.at[n], field_out.at[n], field_sem.at[n])
+
     def finish(n, carry):
         for z, value in enumerate(window(n, me_s * D, True, D)):
             for c in range(6):
                 field_ref[n, c, pl.ds(z, HY, stride=D), :] = value[c]
+        field_copy(n).start()
         return carry
 
     lax.fori_loop(0, NS, finish, 0)
@@ -414,6 +421,8 @@
     offset = lax.rem((me_s * C + me_c) * W, HX)
     surf_ref[...] = pltpu.roll(total, lax.rem(HX - offset, HX), 2)
 
+    for n in range(NS):
+        field_copy(n).wait()
     for copy in surf_sends:
         copy.wait_send()
     for pair in sends:
@@ -443,8 +452,10 @@
             jax.ShapeDtypeStruct((3, NTP, HX), F32),
         ),
         in_specs=[pl.BlockSpec(memory_space=pltpu.HBM)] * 8,
-        out_specs=(vmem, vmem),
+        out_specs=(pl.BlockSpec(memory_space=pltpu.HBM), vmem),
         scratch_shapes=[
+            pltpu.VMEM((NS, 6, HY * D, HX), F32),
+            pltpu.SemaphoreType.DMA((NS,)),
             pltpu.VMEM(tile, F32),
             pltpu.VMEM(tile, jnp.int32),
             pltpu.SMEM((L,), F32),
@@ -474,7 +485,7 @@
             pltpu.SemaphoreType.DMA((C,)),
         ],
         compiler_params=pltpu.CompilerParams(
-            collective_id=0, has_side_effects=True, vmem_limit_bytes=48 * 1024 * 1024
+            collective_id=0, has_side_effects=True, vmem_limit_bytes=60 * 1024 * 1024
         ),
     )(
         body,

time: 22.8 us -> 22.3 us (0.978)
  local copies, waits for them, and re-layouts: 4.21 us -> 3.05 us
  Pallas kernels: 17.6 us -> 18.3 us
    unnamed x18 -> x2, local copies, waits for them, and re-layouts: 4.21 us -> 2.31 us
    transpose x1, local copies, waits for them, and re-layouts: 0.01 us -> 0.74 us  [per_device(): surf = surf[:, :NT, :W].transpose(1, 0, 2)]
    pallas_call x1, Pallas kernels: 17.6 us -> 18.3 us  [per_device(): pl.pallas_call(functools.partial(kernel, S, C, NS, L, D, NT, W), out_shap...]
where the time goes in v3:
time: 22.3 us; the launch traced here: 22 us
  Pallas kernels  18.3 us (82%)
  local copies, waits for them, and re-layouts  3.05 us (14%)
  between operations  0.64 us (3%)
    pallas_call x1, Pallas kernels, per_device(): pl.pallas_call(functools.partial(kernel, S, C, NS, L, D, NT, W), out_shap...  18.3 us
    unnamed x2, local copies, waits for them, and re-layouts  2.31 us
    transpose x1, local copies, waits for them, and re-layouts, per_device(): surf = surf[:, :NT, :W].transpose(1, 0, 2)  0.74 us

profile of v3, /device:TPU:0, one launch (start us, length us, event | category | flops | bytes accessed | tf_op | source)
XLA Modules:
  0.0 22.0 jit_solution(6116694415977286812)
XLA Ops:
  0.6 18.3 %shard_map.95 = (f32[3,6,32,128]{3,2,1,0:T(8,128)}, f32[3,16,128]{2,1,0:T(8,128)}) custom-call(f32[3,32,128]{2,1,0:T(8,128)} %bitcast.20, f32[8,128]{1,0:T(8,128)} %bitcast.22, s32[8,128]{1,0:T(8,128)} %bitcast.23, s32[32,128]{1,0:T(8,128)} %bitcast.21, f32[4]{0:T(128)} %shear_in.1, f32[4]{0:T(128)} %relax_in.1, s32[3]{0:T(128)} %node_in.1, s32[12]{0:T(128)} %time_in.1), custom_call_target="tpu_custom_call" | custom-call | tf_op jit(solution)/shard_map/pallas_call | solution.py:448
  18.9 0.7 %slice_bitcast_fusion = f32[12,3,64]{2,0,1:T(8,128)S(1)} fusion(f32[3,16,128]{2,1,0:T(8,128)} %get-tuple-element.5), kind=kLoop, calls=%fused_computation | loop fusion | bytes 18432 | tf_op jit(solution)/shard_map/transpose | solution.py:501
  19.7 0.6 %copy.13 = f32[12,3,64]{2,1,0:T(4,128)} copy(f32[12,3,64]{2,0,1:T(8,128)S(1)} %slice_bitcast_fusion) | data formatting | bytes 18432
  20.3 1.7 %copy.15 = f32[3,6,4,1024]{3,2,1,0:T(4,128)} copy(f32[3,6,4,1024]{3,2,1,0:T(4,128)} %bitcast.19) | data formatting | bytes 589824
